TPU v7x, 32 devices: a whole 2x2x4 slice. The times are simulated.
32 devices in a mesh: dp: 2 (over x), expert: 16 (over z, y, core).
Axes of the slice: x: 2, y: 2, z: 4, core: 2. Of those that a mesh axis runs over, the one named last changes fastest.
Arguments:
- tokens: bfloat16 [256, 4096], P(('dp', 'expert')), may hold values from -6 to 6
- cotangent: bfloat16 [256, 4096], P(('dp', 'expert')), may hold values from -6 to 6
- gates: float32 [256, 8], P(('dp', 'expert')), may hold values from 0.1 to 0.5
- expert_ids: int32 [256, 8], P(('dp', 'expert')), may hold values from 0 to 15, all different within a row; in each aligned block of 8 rows (0 to 7, 8 to 15, ...) at most 8 rows name the same one
- swap_flag: int32 [16], replicated, may hold values from 0 to 1, as said below
- w_in: bfloat16 [16, 2, 768, 4096], P('expert', None, 'dp'), may hold values from -0.09375 to 0.09375
- w_down: bfloat16 [16, 768, 4096], P('expert', 'dp'), may hold values from -0.21875 to 0.21875
Outputs:
- mixed: bfloat16 [256, 4096], P(('dp', 'expert'))
- grad_tokens: bfloat16 [256, 4096], P(('dp', 'expert'))
- grad_in: bfloat16 [16, 2, 768, 4096], P('expert', None, 'dp')
- grad_down: bfloat16 [16, 768, 4096], P('expert', 'dp')
Inputs may be any that keep to these rules, and one draw needn't show every extreme that they name: `expert_ids`: each row names 8 different experts; in the rows of one device no expert is named more than 8 times. swap_flag[e] equals swap_flag[(e + 8) mod 16]; both values occur.
All inputs are finite; a program needn't handle non-finite values.
Results may differ from a plain program's by a relative error of at most 0.014.
Values may be sent and summed in bfloat16 or wider, within the bound.
No kernel may reach another device: no remote copies, remote signals or barrier semaphores. Data moves between devices by JAX's collectives and lax.ppermute only.
A program may use at most 128 MiB of HBM per device.

v0:
```python
import functools

import jax
import jax.numpy as jnp
from jax import lax
from jax.experimental import pallas as pl
from jax.experimental.pallas import tpu as pltpu
from jax.sharding import PartitionSpec as P

F32, BF16 = jnp.float32, jnp.bfloat16
ANY = pl.BlockSpec(memory_space=pl.ANY)
SMEM = pl.BlockSpec(memory_space=pltpu.SMEM)
VMEM = pl.BlockSpec(memory_space=pltpu.VMEM)
CHUNKS = 4
ROW_BLOCK = 256
STAGE_MIB = 40


def nt(a, b):
    return lax.dot_general(a, b, (((1,), (1,)), ((), ())), preferred_element_type=F32)


def nn(a, b):
    return jnp.dot(a, b, preferred_element_type=F32)


def each_rows(total, body):
    if total <= ROW_BLOCK:
        body(pl.ds(0, total))
    else:

        @pl.loop(0, total // ROW_BLOCK)
        def _(i):
            body(pl.ds(pl.multiple_of(i * ROW_BLOCK, ROW_BLOCK), ROW_BLOCK))


def columns(dim):
    step = dim // CHUNKS
    return [pl.ds(c * step, step) for c in range(CHUNKS)]


def started(sems, base, pairs):
    copies = [
        pltpu.make_async_copy(source, target, sems.at[base + i])
        for i, (source, target) in enumerate(pairs)
    ]
    for copy in copies:
        copy.start()
    return copies


def wait(copies):
    for copy in copies:
        copy.wait()


def row_copies(own, received, buffer, cols, target=None):
    half = own.shape[0]
    target = cols if target is None else target
    return [
        (own.at[:, cols], buffer.at[pl.ds(0, half), target]),
        (received.at[:, cols], buffer.at[pl.ds(half, half), target]),
    ]


def split_three(x):
    high = x.astype(BF16)
    rest = x - high.astype(F32)
    middle = rest.astype(BF16)
    low = (rest - middle.astype(F32)).astype(BF16)
    return high, middle, low


def gate_column(parts, expert, experts):
    lane = lax.broadcasted_iota(jnp.int32, parts.shape, 1)
    values = parts.astype(F32)
    high, middle, low = (
        jnp.sum(jnp.where(lane == expert + i * experts, values, 0.0), axis=1, keepdims=True)
        for i in range(3)
    )
    return (low + middle) + high


def fill_gates(parts, gate, expert, experts):
    def body(rows):
        column = gate_column(parts[rows, :], expert, experts)
        gate[rows, :] = jnp.broadcast_to(column, (column.shape[0], gate.shape[1]))

    each_rows(parts.shape[0], body)


def held_expert(flags):
    me = lax.axis_index("expert")
    flag = flags[me]
    return me, jnp.where(flag > 0, me ^ (lax.axis_size("expert") // 2), me), flag


def stage_kernel(*refs):
    weight, out, sems = refs[-3:]
    wait(started(sems, 0, [(weight.at[:, c], out.at[:, c]) for c in columns(weight.shape[1])]))


def zero_kernel(*refs):
    refs[-1][...] = jnp.zeros_like(refs[-1])


def hidden_kernel(xa, xb, win, after, act, silu, slope, x, hidden, sems):
    units, rows_all = act.shape
    dim = win.shape[1]
    loads = []
    for c, cols in enumerate(columns(dim)):
        loads.append(started(sems, 2 * c, row_copies(xa, xb, x, cols)))
    for c, cols in enumerate(columns(dim)):
        wait(loads[c])

        def multiply(rows):
            product = nt(win[:, cols], x[rows, cols])
            hidden[:, rows] = product if c == 0 else hidden[:, rows] + product

        each_rows(rows_all, multiply)

    def pointwise(rows):
        g, u = hidden[pl.ds(0, units), rows], hidden[pl.ds(units, units), rows]
        sig = jax.nn.sigmoid(g)
        gated = g * sig
        silu[:, rows] = gated
        slope[:, rows] = u * sig * (1.0 + g * (1.0 - sig))
        act[:, rows] = (gated * u).astype(BF16)

    each_rows(rows_all, pointwise)


def split_product(rows_ref, weight, keep, send, finish):
    half, dim = send.shape
    for cols in columns(dim):

        def multiply(start, target):
            def body(rows):
                mine = pl.ds(rows.start + start, rows.size)
                product = nn(rows_ref[mine, :], weight[:, cols]).astype(BF16)
                target[rows, cols] = finish(mine, product)

            return body

        each_rows(half, multiply(half, send))
        each_rows(half, multiply(0, keep))


def part_kernel(
    experts, flags, xa, xb, act, wdown, keep, send, gate, gate_held, parts, rows_act, sems
):
    dim = wdown.shape[1]
    rows_all, width = parts.shape
    loads = started(sems, 0, row_copies(xa, xb, parts, pl.ds(dim, width), pl.ds(0, width)))

    def turn(rows):
        rows_act[rows, :] = act[:, rows].T

    each_rows(rows_all, turn)
    me, held, _ = held_expert(flags)
    wait(loads)
    fill_gates(parts, gate, me, experts)
    fill_gates(parts, gate_held, held, experts)

    def weighted(rows, part):
        return (gate[rows, pl.ds(0, 1)] * part.astype(F32)).astype(BF16)

    split_product(rows_act, wdown, keep, send, weighted)


def back_kernel(factors, win, after, keep, send, rows_grad):
    units = win.shape[0] // 2

    def turn(rows):
        rows_grad[rows, :] = factors[pl.ds(units, 2 * units), rows].T

    each_rows(rows_grad.shape[0], turn)
    split_product(rows_grad, win, keep, send, lambda rows, part: part)


def factor_kernel(
    ya, yb, act, silu, slope, gate, wdown, after, factors, y, total, sems
):
    units, dim = wdown.shape
    rows_all = y.shape[0]
    loads = []
    for c, cols in enumerate(columns(dim)):
        loads.append(started(sems, 2 * c, row_copies(ya, yb, y, cols)))
    factors[pl.ds(0, units), :] = act[...]
    for c, cols in enumerate(columns(dim)):
        wait(loads[c])

        def multiply(rows):
            scaled = (gate[rows, pl.ds(0, 1)] * y[rows, cols].astype(F32)).astype(BF16)
            product = nt(wdown[:, cols], scaled)
            total[:, rows] = product if c == 0 else total[:, rows] + product

        each_rows(rows_all, multiply)

    def pointwise(rows):
        value = total[:, rows]
        factors[pl.ds(units, units), rows] = (value * slope[:, rows]).astype(BF16)
        factors[pl.ds(2 * units, units), rows] = (value * silu[:, rows]).astype(BF16)

    each_rows(rows_all, pointwise)


def weight_kernel(first, scaled, flags, own, away, gate, ra, rb, *rest):
    grads, r, used, out, sems = rest[-5:]
    groups, units, dim = grads.shape
    rows_all = r.shape[0]
    base, loads, stores = 0, [], []
    for cols in columns(dim):
        loads.append(started(sems, base, row_copies(ra, rb, r, cols)))
        base += 2
    _, _, flag = held_expert(flags)
    some = pl.ds(first * units, groups * units)
    used[...] = jnp.where(flag > 0, away[some, :], own[some, :])
    for c, cols in enumerate(columns(dim)):
        wait(loads[c])
        if scaled:

            def scale(rows):
                r[rows, cols] = (gate[rows, pl.ds(0, 1)] * r[rows, cols].astype(F32)).astype(BF16)

            each_rows(rows_all, scale)
        pairs = []
        for i in range(groups):
            some = pl.ds(i * units, units)
            out[some, cols] = nn(used[some, :], r[:, cols]).astype(BF16)
            pairs.append((out.at[some, cols], grads.at[i, :, cols]))
        stores.append(started(sems, base, pairs))
        base += groups
    for store in stores:
        wait(store)


def rounded_up(value, unit):
    return -(-value // unit) * unit


def params(mib):
    return pltpu.CompilerParams(vmem_limit_bytes=mib * 1024 * 1024)


def cost(flops, size):
    return pl.CostEstimate(flops=flops, bytes_accessed=size, transcendentals=0)


def masks(axis):
    size, out = lax.axis_size(axis), []
    while size > 1:
        size //= 2
        out.append((axis, size))
    return out


def partner(block, bit):
    axis, mask = bit
    return lax.ppermute(block, axis, [(i, i ^ mask) for i in range(lax.axis_size(axis))])


def inner_rows(bit, done, order, unit):
    for other in done:
        if order.index(other) > order.index(bit):
            unit *= 2
    return unit


def join(a, b, inner):
    pair = [part.reshape(-1, inner, part.shape[-1]) for part in (a, b)]
    return jnp.concatenate(pair, axis=1).reshape(-1, a.shape[-1])


def halves(block, inner):
    split = block.reshape(-1, 2, inner, block.shape[1])
    return [split[:, i].reshape(-1, block.shape[1]) for i in (0, 1)]


def is_set(bit):
    return (lax.axis_index(bit[0]) & bit[1]) > 0


def add(a, b):
    return (a.astype(F32) + b.astype(F32)).astype(BF16)


def on_device(tokens, cotangent, gates, expert_ids, swap_flag, w_in, w_down):
    experts = lax.axis_size("expert")
    half_axis = experts // 2
    tok_dev, dim = tokens.shape
    units = w_down.shape[1]

    across, within = masks("dp"), masks("expert")
    core, near, far = within[-1], within[-2:-1], within[:-2]
    first = near + across
    second = across + near
    order = first[::-1] + far[::-1]
    rows_all = tok_dev * lax.axis_size("dp") * experts
    top = far[0]

    slots = jnp.arange(experts, dtype=jnp.int32)
    dense = jnp.sum(
        jnp.where(expert_ids[:, :, None] == slots, gates[:, :, None], 0.0), axis=1
    )
    parts = jnp.concatenate(split_three(dense), axis=1)
    width = rounded_up(parts.shape[1], 128)
    parts = jnp.pad(parts, ((0, 0), (0, width - parts.shape[1])))
    payload = jnp.stack([jnp.concatenate([rows, parts], axis=1) for rows in (tokens, cotangent)])

    def far_gather(block):
        for i in range(0, len(far), 2):
            group = far[i : i + 2]

            def arrived(rows, bit):
                return partner(rows.reshape(-1, rows.shape[2]), bit).reshape(rows.shape)

            a = group[0]
            across = arrived(block, a)
            if len(group) == 2:
                b = group[1]
                pairs = [jnp.concatenate([rows, arrived(rows, b)], axis=1) for rows in (block, across)]
            else:
                pairs = [block, across]
            if a == top:
                turn = is_set(top)
                pairs = [jnp.where(turn, pairs[1 - j], pairs[j]) for j in (0, 1)]
            block = jnp.concatenate(pairs, axis=1)
        return block

    def plane_step_out(rows, route, k, zero=None):
        got = partner(rows, route[k])
        got = got if zero is None else got + zero
        return join(rows, got, inner_rows(route[k], route[:k], order, far_rows))

    def zero_after(columns_of, *arrays):
        return pl.pallas_call(
            zero_kernel,
            out_shape=jax.ShapeDtypeStruct((16, columns_of), BF16),
            in_specs=[ANY] * len(arrays),
            out_specs=VMEM,
            compiler_params=params(2),
            name="zero",
        )(*arrays)[:1]

    def stage(weight, after, name):
        return pl.pallas_call(
            stage_kernel,
            out_shape=jax.ShapeDtypeStruct(weight.shape, BF16),
            in_specs=[ANY] * (len(after) + 1),
            out_specs=VMEM,
            scratch_shapes=[pltpu.SemaphoreType.DMA((CHUNKS,))],
            compiler_params=params(STAGE_MIB),
            cost_estimate=cost(0, 4 * weight.size),
            name=name,
        )(*after, weight)

    x_far, y_far = far_gather(payload)
    far_rows = x_far.shape[0]
    xa, ya = x_far, y_far
    for k in range(len(first)):
        zero = None
        if k == len(first) - 1:
            win = stage(w_in.reshape(2 * units, dim), (xa, ya), "stage_in")
            wdown = stage(w_down.reshape(units, dim), (xa, ya), "stage_down")
            zero = zero_after(dim + width, win, wdown)
        xa, ya = plane_step_out(xa, first, k, zero), plane_step_out(ya, second, k)
    xb, yb = partner(xa, core), partner(ya, core)

    half_rows = rows_all // 2
    limit = 60 if rows_all > 512 else 24
    row_type = jax.ShapeDtypeStruct((half_rows, dim), BF16)
    gate_type = jax.ShapeDtypeStruct((rows_all, 128), F32)
    saved_type = jax.ShapeDtypeStruct((units, rows_all), F32)
    product = 2 * rows_all * units * dim
    act, silu, slope = pl.pallas_call(
        hidden_kernel,
        out_shape=[
            jax.ShapeDtypeStruct((units, rows_all), BF16),
            saved_type,
            saved_type,
        ],
        in_specs=[ANY, ANY, VMEM, ANY],
        out_specs=[VMEM] * 3,
        scratch_shapes=[
            pltpu.VMEM((rows_all, dim), BF16),
            pltpu.VMEM((2 * units, rows_all), F32),
            pltpu.SemaphoreType.DMA((2 * CHUNKS,)),
        ],
        compiler_params=params(limit),
        cost_estimate=cost(2 * product, 4 * dim * (units + rows_all)),
        name="hidden",
    )(xa, xb, win, wdown)
    mixed_keep, mixed_send, gate, gate_held = pl.pallas_call(
        functools.partial(part_kernel, experts),
        out_shape=[row_type, row_type, gate_type, gate_type],
        in_specs=[SMEM, ANY, ANY, VMEM, VMEM],
        out_specs=[VMEM] * 4,
        scratch_shapes=[
            pltpu.VMEM((rows_all, width), BF16),
            pltpu.VMEM((rows_all, units), BF16),
            pltpu.SemaphoreType.DMA((2,)),
        ],
        compiler_params=params(limit),
        cost_estimate=cost(product, 2 * dim * (units + rows_all)),
        name="part",
    )(swap_flag, xa, xb, act, wdown)
    factors = pl.pallas_call(
        factor_kernel,
        out_shape=jax.ShapeDtypeStruct((3 * units, rows_all), BF16),
        in_specs=[ANY] * 2 + [VMEM] * 5 + [ANY],
        out_specs=VMEM,
        scratch_shapes=[
            pltpu.VMEM((rows_all, dim), BF16),
            pltpu.VMEM((units, rows_all), F32),
            pltpu.SemaphoreType.DMA((2 * CHUNKS,)),
        ],
        compiler_params=params(limit),
        cost_estimate=cost(product, 2 * dim * (units + rows_all)),
        name="factors",
    )(ya, yb, act, silu, slope, gate, wdown, mixed_send)
    far_factors = partner(factors, ("expert", half_axis))
    mixed_got = partner(mixed_send, core)
    back_keep, back_send = pl.pallas_call(
        back_kernel,
        out_shape=[row_type, row_type],
        in_specs=[VMEM] * 2 + [ANY],
        out_specs=[VMEM] * 2,
        scratch_shapes=[pltpu.VMEM((rows_all, 2 * units), BF16)],
        compiler_params=params(limit),
        cost_estimate=cost(2 * product, 4 * dim * (units + rows_all)),
        name="back",
    )(factors, win, mixed_got)

    def added(keep, got, bit, left):
        inner = inner_rows(bit, left, order, tok_dev)
        return [add(*pair) for pair in zip(halves(keep, inner), halves(got, inner))]

    def far_sum(rows, group, late=None):
        a = group[0]
        inner = rows.shape[0] // 2
        pair = [rows[:inner], rows[inner:]]
        if a == top:
            turn = is_set(top)
            pair = [jnp.where(turn, pair[1 - j], pair[j]) for j in (0, 1)]
        if len(group) == 1:
            onward = pair[1] if late is None else pair[1] + late(pair[1])
            return add(pair[0], partner(onward, a)), onward
        b = group[1]
        low = inner // 2
        furthest, beside = pair[1][low:], pair[0][low:]
        onward = add(pair[1][:low], partner(furthest, b))
        if late is not None:
            onward = onward + late(furthest, beside)
        total = pair[0][:low].astype(F32) + partner(beside, b).astype(F32)
        return (total + partner(onward, a).astype(F32)).astype(BF16), onward

    groups = [far[i : i + 2] for i in range(0, len(far), 2)]

    def plane_step(keep, got, route, k):
        left = set(order) - set(route[: k + 1])
        keep, sent = added(keep, got, route[k], left)
        return keep, partner(sent, route[k]), sent

    def weight_gradient(after, first, groups, pieces, scaled, name):
        return pl.pallas_call(
            functools.partial(weight_kernel, first, scaled),
            out_shape=jax.ShapeDtypeStruct((groups, units, dim), BF16),
            in_specs=[SMEM] + [VMEM] * 3 + [ANY] * (2 + len(after)),
            out_specs=ANY,
            scratch_shapes=[
                pltpu.VMEM((rows_all, dim), BF16),
                pltpu.VMEM((groups * units, rows_all), BF16),
                pltpu.VMEM((groups * units, dim), BF16),
                pltpu.SemaphoreType.DMA(((2 + groups) * CHUNKS,)),
            ],
            compiler_params=params(limit),
            cost_estimate=cost(groups * product, 2 * dim * (groups * units + rows_all)),
            name=name,
        )(swap_flag, factors, far_factors, gate_held, *pieces, *after)

    across_first, near_first = first[::-1], second[::-1]
    back_got = partner(back_send, core)
    for k in range(len(first)):
        if k > 0:
            mixed_got = mixed_got + zero_after(dim, back_sent)
        mixed_keep, mixed_got, mixed_sent = plane_step(mixed_keep, mixed_got, across_first, k)
        back_keep, back_got, back_sent = plane_step(back_keep, back_got, near_first, k)
    both = jnp.concatenate([add(mixed_keep, mixed_got), add(back_keep, back_got)], axis=1)
    for group in groups[:0:-1]:
        both, _ = far_sum(both, group)
    both, sent = far_sum(both, groups[0], lambda *ahead: zero_after(2 * dim, far_factors, *ahead))
    mixed, grad_tokens = both[:, :dim], both[:, dim:]
    behind = [sent]
    new_down = weight_gradient(behind, 0, 1, (ya, yb), True, "grad_down")
    new_in = weight_gradient(behind, 1, 2, (xa, xb), False, "grad_in")
    return (mixed, grad_tokens, new_in.reshape(w_in.shape), new_down.reshape(w_down.shape))


def solution(mesh):
    rows = P(("dp", "expert"), None)
    w_in, w_down = P("expert", None, "dp", None), P("expert", "dp", None)
    return jax.shard_map(
        on_device,
        mesh=mesh,
        in_specs=(rows, rows, rows, rows, P(), w_in, w_down),
        out_specs=(rows, rows, w_in, w_down),
        check_vma=False,
    )
```

profile of v0, /device:TPU:0, one launch (start us, length us, event | category | flops | bytes accessed | tf_op | source)
XLA Modules:
  0.0 95.5 jit_solution(16979796133278653157)
XLA Ops:
  2.4 4.1 %collective-permute-start = (bf16[16,4224]{1,0:T(8,128)(2,1)S(1)}, bf16[16,4224]{1,0:T(8,128)(2,1)S(1)}, u32[]{:S(2)}, u32[]{:S(2)}) collective-permute-start(bf16[16,4224]{1,0:T(8,128)(2,1)S(1)} %maximum_bitcast_fusion.2), channel_id=1, source_target_pairs={{0,8},{1,9},{2,10},{3,11},{4,12},{5,13},{6,14},{7,15},{8,0},{9,1},... | collective-permute-start | bytes 405512 | tf_op jit(solution)/shard_map/ppermute | solution.py:260
  6.5 1.6 %collective-permute-start.2 = (bf16[16,4224]{1,0:T(8,128)(2,1)S(1)}, bf16[16,4224]{1,0:T(8,128)(2,1)S(1)}, u32[]{:S(2)}, u32[]{:S(2)}) collective-permute-start(bf16[16,4224]{1,0:T(8,128)(2,1)S(1)} %maximum_bitcast_fusion.2), channel_id=1, source_target_pairs={{0,4},{1,5},{2,6},{3,7},{4,0},{5,1},{6,2},{7,3},{8,12},{9,13},{10,... | collective-permute-start | bytes 405512 | tf_op jit(solution)/shard_map/ppermute | solution.py:260
  8.1 5.0 %collective-permute-done = bf16[16,4224]{1,0:T(8,128)(2,1)S(1)} collective-permute-done((bf16[16,4224]{1,0:T(8,128)(2,1)S(1)}, bf16[16,4224]{1,0:T(8,128)(2,1)S(1)}, u32[]{:S(2)}, u32[]{:S(2)}) %collective-permute-start) | collective-permute-done | bytes 135200 | tf_op jit(solution)/shard_map/ppermute | solution.py:260
  13.7 4.4 %collective-permute-done.1 = bf16[16,4224]{1,0:T(8,128)(2,1)S(1)} collective-permute-done((bf16[16,4224]{1,0:T(8,128)(2,1)S(1)}, bf16[16,4224]{1,0:T(8,128)(2,1)S(1)}, u32[]{:S(2)}, u32[]{:S(2)}) %collective-permute-start.1) | collective-permute-done | bytes 135200 | tf_op jit(solution)/shard_map/ppermute | solution.py:260
  18.3 1.6 %collective-permute-start.3 = (bf16[32,4224]{1,0:T(8,128)(2,1)S(1)}, bf16[32,4224]{1,0:T(8,128)(2,1)S(1)}, u32[]{:S(2)}, u32[]{:S(2)}) collective-permute-start(bf16[32,4224]{1,0:T(8,128)(2,1)S(1)} %bitcast.73), channel_id=1, source_target_pairs={{0,2},{1,3},{2,0},{3,1},{4,6},{5,7},{6,4},{7,5},{8,10},{9,11},{10,... | collective-permute-start | bytes 811016 | tf_op jit(solution)/shard_map/ppermute | solution.py:260
  21.4 3.4 %collective-permute-done.3 = bf16[32,4224]{1,0:T(8,128)(2,1)S(1)} collective-permute-done((bf16[32,4224]{1,0:T(8,128)(2,1)S(1)}, bf16[32,4224]{1,0:T(8,128)(2,1)S(1)}, u32[]{:S(2)}, u32[]{:S(2)}) %collective-permute-start.3) | collective-permute-done | bytes 270368 | tf_op jit(solution)/shard_map/ppermute | solution.py:260
  24.9 1.6 %collective-permute-start.4 = (bf16[64,4224]{1,0:T(8,128)(2,1)S(1)}, bf16[64,4224]{1,0:T(8,128)(2,1)S(1)}, u32[]{:S(2)}, u32[]{:S(2)}) collective-permute-start(bf16[64,4224]{1,0:T(8,128)(2,1)S(1)} %maximum_bitcast_fusion.1.refs_0_), channel_id=1, source_target_pairs={{0,16},{16,0},{1,17},{17,1},{2,18},{18,2},{3,19},{19,3},{4,20},{20... | collective-permute-start | bytes 1622024 | tf_op jit(solution)/shard_map/ppermute | solution.py:260
  26.5 2.1 %collective-permute-done.5 = bf16[32,4224]{1,0:T(8,128)(2,1)S(1)} collective-permute-done((bf16[32,4224]{1,0:T(8,128)(2,1)S(1)}, bf16[32,4224]{1,0:T(8,128)(2,1)S(1)}, u32[]{:S(2)}, u32[]{:S(2)}) %collective-permute-start.5) | collective-permute-done | bytes 270368 | tf_op jit(solution)/shard_map/ppermute | solution.py:260
  29.2 2.4 %copy-done = bf16[1,2,384,4096]{3,2,1,0:T(8,128)(2,1)S(1)} copy-done((bf16[1,2,384,4096]{3,2,1,0:T(8,128)(2,1)S(1)}, bf16[1,2,384,4096]{3,2,1,0:T(8,128)(2,1)}, u32[]{:S(2)}) %copy-start) | copy-done | bytes 6291480
  31.5 1.6 %stage_in.1.refs_0_.win = bf16[768,4096]{1,0:T(8,128)(2,1)S(1)} custom-call(bf16[64,4224]{1,0:T(8,128)(2,1)S(1)} %maximum_bitcast_fusion.1.refs_0_, bf16[64,4224]{1,0:T(8,128)(2,1)S(1)} %get-tuple-element.27.refs_1_, bf16[768,4096]{1,0:T(8,128)(2,1)S(1)} %bitcast.64), custom_call_target="tpu_custom_call" | custom-call | bytes 12582912 | tf_op jit(solution)/shard_map/stage_in/pallas_call | solution.py:347
  33.2 4.8 %collective-permute-done.4 = bf16[64,4224]{1,0:T(8,128)(2,1)S(1)} collective-permute-done((bf16[64,4224]{1,0:T(8,128)(2,1)S(1)}, bf16[64,4224]{1,0:T(8,128)(2,1)S(1)}, u32[]{:S(2)}, u32[]{:S(2)}) %collective-permute-start.4) | collective-permute-done | bytes 540704 | tf_op jit(solution)/shard_map/ppermute | solution.py:260
  38.9 2.0 %collective-permute-done.6.xb.rb = bf16[128,4224]{1,0:T(8,128)(2,1)S(1)} collective-permute-done((bf16[128,4224]{1,0:T(8,128)(2,1)S(1)}, bf16[128,4224]{1,0:T(8,128)(2,1)S(1)}, u32[]{:S(2)}, u32[]{:S(2)}) %collective-permute-start.6) | collective-permute-done | bytes 1081376 | tf_op jit(solution)/shard_map/ppermute | solution.py:260
  40.9 4.0 %hidden.1 = (bf16[384,256]{1,0:T(8,128)(2,1)S(1)}, f32[384,256]{1,0:T(8,128)S(1)}, f32[384,256]{1,0:T(8,128)S(1)}) custom-call(bf16[128,4224]{1,0:T(8,128)(2,1)S(1)} %maximum_bitcast_fusion.xa.ra, bf16[128,4224]{1,0:T(8,128)(2,1)S(1)} %collective-permute-done.6.xb.rb, bf16[768,4096]{1,0:T(8,128)(2,1)S(1)} %stage_in.1.refs_0_.win, ...), custom_call_target="tpu_custom_call" | custom-call | flops 1610612736 | bytes 10485760 | tf_op jit(solution)/shard_map/hidden/pallas_call | solution.py:376
  44.9 2.0 %part.1 = (bf16[128,4096]{1,0:T(8,128)(2,1)S(1)}, bf16[128,4096]{1,0:T(8,128)(2,1)S(1)}, f32[256,128]{1,0:T(8,128)S(1)}, f32[256,128]{1,0:T(8,128)S(1)}) custom-call(s32[16]{0:T(128)S(1)} %copy-done.2, bf16[128,4224]{1,0:T(8,128)(2,1)S(1)} %maximum_bitcast_fusion.xa.ra, bf16[128,4224]{1,0:T(8,128)(2,1)S(1)} %collective-permute-done.6.xb.rb, ...), custom_call_target="tpu_custom_call" | custom-call | flops 805306368 | bytes 5242880 | tf_op jit(solution)/shard_map/part/pallas_call | solution.py:394
  47.1 2.6 %factors.1.own = bf16[1152,256]{1,0:T(8,128)(2,1)S(1)} custom-call(bf16[128,4224]{1,0:T(8,128)(2,1)S(1)} %bitcast.62, bf16[128,4224]{1,0:T(8,128)(2,1)S(1)} %collective-permute-done.10.yb.rb, bf16[384,256]{1,0:T(8,128)(2,1)S(1)} %get-tuple-element.13.act, f32[384,256]{1,0:T(8,128)S(1)} %get-tuple-element.16.silu, f32[384,256]{1,0:T(8,128)S(1)} %get-tuple-element.17.slope, ...), custom_call_target="tpu_custom_call" | custom-call | flops 805306368 | bytes 5242880 | tf_op jit(solution)/shard_map/factors/pallas_call | solution.py:408
  49.8 1.8 %back.1 = (bf16[128,4096]{1,0:T(8,128)(2,1)S(1)}, bf16[128,4096]{1,0:T(8,128)(2,1)S(1)}) custom-call(bf16[1152,256]{1,0:T(8,128)(2,1)S(1)} %factors.1.own, bf16[768,4096]{1,0:T(8,128)(2,1)S(1)} %stage_in.1.refs_0_.win, bf16[128,4096]{1,0:T(8,128)(2,1)S(1)} %collective-permute-done.7.after), custom_call_target="tpu_custom_call" | custom-call | flops 1610612736 | bytes 10485760 | tf_op jit(solution)/shard_map/back/pallas_call | solution.py:424
  52.1 3.9 %collective-permute-start.17 = (bf16[1152,256]{1,0:T(8,128)(2,1)S(1)}, bf16[1152,256]{1,0:T(8,128)(2,1)S(1)}, u32[]{:S(2)}, u32[]{:S(2)}) collective-permute-start(bf16[1152,256]{1,0:T(8,128)(2,1)S(1)} %factors.1.own), channel_id=1, source_target_pairs={{0,8},{1,9},{2,10},{3,11},{4,12},{5,13},{6,14},{7,15},{8,0},{9,1},... | collective-permute-start | bytes 1769480 | tf_op jit(solution)/shard_map/ppermute | solution.py:260
  57.9 1.6 %collective-permute-start.13 = (bf16[64,4096]{1,0:T(8,128)(2,1)S(1)}, bf16[64,4096]{1,0:T(8,128)(2,1)S(1)}, u32[]{:S(2)}, u32[]{:S(2)}) collective-permute-start(bf16[64,4096]{1,0:T(8,128)(2,1)S(1)} %bitcast.68), channel_id=1, source_target_pairs={{0,2},{1,3},{2,0},{3,1},{4,6},{5,7},{6,4},{7,5},{8,10},{9,11},{10,... | collective-permute-start | bytes 1572872 | tf_op jit(solution)/shard_map/ppermute | solution.py:260
  59.6 10.4 %collective-permute-done.8 = bf16[64,4096]{1,0:T(8,128)(2,1)S(1)} collective-permute-done((bf16[64,4096]{1,0:T(8,128)(2,1)S(1)}, bf16[64,4096]{1,0:T(8,128)(2,1)S(1)}, u32[]{:S(2)}, u32[]{:S(2)}) %collective-permute-start.8) | collective-permute-done | bytes 524320 | tf_op jit(solution)/shard_map/ppermute | solution.py:260
  70.1 1.6 %collective-permute-start.12 = (bf16[32,4096]{1,0:T(8,128)(2,1)S(1)}, bf16[32,4096]{1,0:T(8,128)(2,1)S(1)}, u32[]{:S(2)}, u32[]{:S(2)}) collective-permute-start(bf16[32,4096]{1,0:T(8,128)(2,1)S(1)} %fusion.6), channel_id=1, source_target_pairs={{0,2},{1,3},{2,0},{3,1},{4,6},{5,7},{6,4},{7,5},{8,10},{9,11},{10,... | collective-permute-start | bytes 786440 | tf_op jit(solution)/shard_map/ppermute | solution.py:260
  73.5 3.9 %collective-permute-done.12 = bf16[32,4096]{1,0:T(8,128)(2,1)S(1)} collective-permute-done((bf16[32,4096]{1,0:T(8,128)(2,1)S(1)}, bf16[32,4096]{1,0:T(8,128)(2,1)S(1)}, u32[]{:S(2)}, u32[]{:S(2)}) %collective-permute-start.12) | collective-permute-done | bytes 262176 | tf_op jit(solution)/shard_map/ppermute | solution.py:260
  82.4 3.2 %collective-permute-done.16 = bf16[8,8192]{1,0:T(8,128)(2,1)S(1)} collective-permute-done((bf16[8,8192]{1,0:T(8,128)(2,1)S(1)}, bf16[8,8192]{1,0:T(8,128)(2,1)S(1)}, u32[]{:S(2)}, u32[]{:S(2)}) %collective-permute-start.16) | collective-permute-done | bytes 131104 | tf_op jit(solution)/shard_map/ppermute | solution.py:260
  86.8 3.7 %grad_down.1 = bf16[1,384,4096]{2,1,0:T(8,128)(2,1)} custom-call(s32[16]{0:T(128)S(1)} %copy-done.2, bf16[1152,256]{1,0:T(8,128)(2,1)S(1)} %factors.1.own, bf16[1152,256]{1,0:T(8,128)(2,1)S(1)} %collective-permute-done.17.refs_0_.away, f32[256,128]{1,0:T(8,128)S(1)} %get-tuple-element.21.gate, bf16[128,4224]{1,0:T(8,128)(2,1)S(1)} %bitcast.63, ...), custom_call_target="tpu_custom_call" | custom-call | flops 805306368 | bytes 5242880 | tf_op jit(solution)/shard_map/grad_down/pallas_call | solution.py:466
  90.5 4.3 %grad_in.1 = bf16[2,384,4096]{2,1,0:T(8,128)(2,1)} custom-call(s32[16]{0:T(128)S(1)} %copy-done.2, bf16[1152,256]{1,0:T(8,128)(2,1)S(1)} %factors.1.own, bf16[1152,256]{1,0:T(8,128)(2,1)S(1)} %collective-permute-done.17.refs_0_.away, f32[256,128]{1,0:T(8,128)S(1)} %get-tuple-element.21.gate, bf16[128,4224]{1,0:T(8,128)(2,1)S(1)} %maximum_bitcast_fusion.xa.ra, ...), custom_call_target="tpu_custom_call" | custom-call | flops 1610612736 | bytes 8388608 | tf_op jit(solution)/shard_map/grad_in/pallas_call | solution.py:466
  (60 shorter events, 17.0 us)
Async XLA Ops:
  2.4 10.7 %collective-permute-start = (bf16[16,4224]{1,0:T(8,128)(2,1)S(1)}, bf16[16,4224]{1,0:T(8,128)(2,1)S(1)}, u32[]{:S(2)}, u32[]{:S(2)}) collective-permute-start(bf16[16,4224]{1,0:T(8,128)(2,1)S(1)} %maximum_bitcast_fusion.2), channel_id=1, source_target_pairs={{0,8},{1,9},{2,10},{3,11},{4,12},{5,13},{6,14},{7,15},{8,0},{9,1},... | collective-permute-start | bytes 405512 | tf_op jit(solution)/shard_map/ppermute | solution.py:260
  6.5 7.2 %collective-permute-start.2 = (bf16[16,4224]{1,0:T(8,128)(2,1)S(1)}, bf16[16,4224]{1,0:T(8,128)(2,1)S(1)}, u32[]{:S(2)}, u32[]{:S(2)}) collective-permute-start(bf16[16,4224]{1,0:T(8,128)(2,1)S(1)} %maximum_bitcast_fusion.2), channel_id=1, source_target_pairs={{0,4},{1,5},{2,6},{3,7},{4,0},{5,1},{6,2},{7,3},{8,12},{9,13},{10,... | collective-permute-start | bytes 405512 | tf_op jit(solution)/shard_map/ppermute | solution.py:260
  13.1 5.0 %collective-permute-start.1 = (bf16[16,4224]{1,0:T(8,128)(2,1)S(1)}, bf16[16,4224]{1,0:T(8,128)(2,1)S(1)}, u32[]{:S(2)}, u32[]{:S(2)}) collective-permute-start(bf16[16,4224]{1,0:T(8,128)(2,1)S(1)} %collective-permute-done), channel_id=1, source_target_pairs={{0,4},{1,5},{2,6},{3,7},{4,0},{5,1},{6,2},{7,3},{8,12},{9,13},{10,... | collective-permute-start | bytes 405512 | tf_op jit(solution)/shard_map/ppermute | solution.py:260
  18.2 10.5 %copy-start.1 = (bf16[1,384,4096]{2,1,0:T(8,128)(2,1)S(1)}, bf16[1,384,4096]{2,1,0:T(8,128)(2,1)}, u32[]{:S(2)}) copy-start(bf16[1,384,4096]{2,1,0:T(8,128)(2,1)} %param.13) | copy-start | bytes 9437188
  18.3 6.5 %collective-permute-start.3 = (bf16[32,4224]{1,0:T(8,128)(2,1)S(1)}, bf16[32,4224]{1,0:T(8,128)(2,1)S(1)}, u32[]{:S(2)}, u32[]{:S(2)}) collective-permute-start(bf16[32,4224]{1,0:T(8,128)(2,1)S(1)} %bitcast.73), channel_id=1, source_target_pairs={{0,2},{1,3},{2,0},{3,1},{4,6},{5,7},{6,4},{7,5},{8,10},{9,11},{10,... | collective-permute-start | bytes 811016 | tf_op jit(solution)/shard_map/ppermute | solution.py:260
  19.9 8.6 %collective-permute-start.5 = (bf16[32,4224]{1,0:T(8,128)(2,1)S(1)}, bf16[32,4224]{1,0:T(8,128)(2,1)S(1)}, u32[]{:S(2)}, u32[]{:S(2)}) collective-permute-start(bf16[32,4224]{1,0:T(8,128)(2,1)S(1)} %bitcast.81), channel_id=1, source_target_pairs={{0,16},{16,0},{1,17},{17,1},{2,18},{18,2},{3,19},{19,3},{4,20},{20... | collective-permute-start | bytes 811016 | tf_op jit(solution)/shard_map/ppermute | solution.py:260
  24.9 13.1 %collective-permute-start.4 = (bf16[64,4224]{1,0:T(8,128)(2,1)S(1)}, bf16[64,4224]{1,0:T(8,128)(2,1)S(1)}, u32[]{:S(2)}, u32[]{:S(2)}) collective-permute-start(bf16[64,4224]{1,0:T(8,128)(2,1)S(1)} %maximum_bitcast_fusion.1.refs_0_), channel_id=1, source_target_pairs={{0,16},{16,0},{1,17},{17,1},{2,18},{18,2},{3,19},{19,3},{4,20},{20... | collective-permute-start | bytes 1622024 | tf_op jit(solution)/shard_map/ppermute | solution.py:260
  28.7 9.5 %collective-permute-start.9 = (bf16[64,4224]{1,0:T(8,128)(2,1)S(1)}, bf16[64,4224]{1,0:T(8,128)(2,1)S(1)}, u32[]{:S(2)}, u32[]{:S(2)}) collective-permute-start(bf16[64,4224]{1,0:T(8,128)(2,1)S(1)} %get-tuple-element.27.refs_1_), channel_id=1, source_target_pairs={{0,2},{1,3},{2,0},{3,1},{4,6},{5,7},{6,4},{7,5},{8,10},{9,11},{10,... | collective-permute-start | bytes 1622024 | tf_op jit(solution)/shard_map/ppermute | solution.py:260
  28.7 2.8 %copy-start = (bf16[1,2,384,4096]{3,2,1,0:T(8,128)(2,1)S(1)}, bf16[1,2,384,4096]{3,2,1,0:T(8,128)(2,1)}, u32[]{:S(2)}) copy-start(bf16[1,2,384,4096]{3,2,1,0:T(8,128)(2,1)} %param.12) | copy-start | bytes 18874372
  38.1 2.8 %collective-permute-start.6 = (bf16[128,4224]{1,0:T(8,128)(2,1)S(1)}, bf16[128,4224]{1,0:T(8,128)(2,1)S(1)}, u32[]{:S(2)}, u32[]{:S(2)}) collective-permute-start(bf16[128,4224]{1,0:T(8,128)(2,1)S(1)} %maximum_bitcast_fusion.xa.ra), channel_id=1, source_target_pairs={{0,1},{1,0},{2,3},{3,2},{4,5},{5,4},{6,7},{7,6},{8,9},{9,8},{10,11... | collective-permute-start | bytes 3244040 | tf_op jit(solution)/shard_map/ppermute | solution.py:260
  38.3 6.6 %copy-start.2 = (s32[16]{0:T(128)S(1)}, s32[16]{0:T(128)}, u32[]{:S(2)}) copy-start(s32[16]{0:T(128)} %flags.5) | copy-start | bytes 196
  38.3 8.8 %collective-permute-start.10 = (bf16[128,4224]{1,0:T(8,128)(2,1)S(1)}, bf16[128,4224]{1,0:T(8,128)(2,1)S(1)}, u32[]{:S(2)}, u32[]{:S(2)}) collective-permute-start(bf16[128,4224]{1,0:T(8,128)(2,1)S(1)} %bitcast.61), channel_id=1, source_target_pairs={{0,1},{1,0},{2,3},{3,2},{4,5},{5,4},{6,7},{7,6},{8,9},{9,8},{10,11... | collective-permute-start | bytes 3244040 | tf_op jit(solution)/shard_map/ppermute | solution.py:260
  46.9 2.9 %collective-permute-start.7 = (bf16[128,4096]{1,0:T(8,128)(2,1)S(1)}, bf16[128,4096]{1,0:T(8,128)(2,1)S(1)}, u32[]{:S(2)}, u32[]{:S(2)}) collective-permute-start(bf16[128,4096]{1,0:T(8,128)(2,1)S(1)} %get-tuple-element.15.after), channel_id=1, source_target_pairs={{0,1},{1,0},{2,3},{3,2},{4,5},{5,4},{6,7},{7,6},{8,9},{9,8},{10,11... | collective-permute-start | bytes 3145736 | tf_op jit(solution)/shard_map/ppermute | solution.py:260
  51.7 6.1 %collective-permute-start.11 = (bf16[128,4096]{1,0:T(8,128)(2,1)S(1)}, bf16[128,4096]{1,0:T(8,128)(2,1)S(1)}, u32[]{:S(2)}, u32[]{:S(2)}) collective-permute-start(bf16[128,4096]{1,0:T(8,128)(2,1)S(1)} %get-tuple-element.20), channel_id=1, source_target_pairs={{0,1},{1,0},{2,3},{3,2},{4,5},{5,4},{6,7},{7,6},{8,9},{9,8},{10,11... | collective-permute-start | bytes 3145736 | tf_op jit(solution)/shard_map/ppermute | solution.py:260
  52.1 30.2 %collective-permute-start.17 = (bf16[1152,256]{1,0:T(8,128)(2,1)S(1)}, bf16[1152,256]{1,0:T(8,128)(2,1)S(1)}, u32[]{:S(2)}, u32[]{:S(2)}) collective-permute-start(bf16[1152,256]{1,0:T(8,128)(2,1)S(1)} %factors.1.own), channel_id=1, source_target_pairs={{0,8},{1,9},{2,10},{3,11},{4,12},{5,13},{6,14},{7,15},{8,0},{9,1},... | collective-permute-start | bytes 1769480 | tf_op jit(solution)/shard_map/ppermute | solution.py:260
  56.2 13.7 %collective-permute-start.8 = (bf16[64,4096]{1,0:T(8,128)(2,1)S(1)}, bf16[64,4096]{1,0:T(8,128)(2,1)S(1)}, u32[]{:S(2)}, u32[]{:S(2)}) collective-permute-start(bf16[64,4096]{1,0:T(8,128)(2,1)S(1)} %get-tuple-element.23), channel_id=1, source_target_pairs={{0,16},{16,0},{1,17},{17,1},{2,18},{18,2},{3,19},{19,3},{4,20},{20... | collective-permute-start | bytes 1572872 | tf_op jit(solution)/shard_map/ppermute | solution.py:260
  57.9 13.9 %collective-permute-start.13 = (bf16[64,4096]{1,0:T(8,128)(2,1)S(1)}, bf16[64,4096]{1,0:T(8,128)(2,1)S(1)}, u32[]{:S(2)}, u32[]{:S(2)}) collective-permute-start(bf16[64,4096]{1,0:T(8,128)(2,1)S(1)} %bitcast.68), channel_id=1, source_target_pairs={{0,2},{1,3},{2,0},{3,1},{4,6},{5,7},{6,4},{7,5},{8,10},{9,11},{10,... | collective-permute-start | bytes 1572872 | tf_op jit(solution)/shard_map/ppermute | solution.py:260
  70.1 7.3 %collective-permute-start.12 = (bf16[32,4096]{1,0:T(8,128)(2,1)S(1)}, bf16[32,4096]{1,0:T(8,128)(2,1)S(1)}, u32[]{:S(2)}, u32[]{:S(2)}) collective-permute-start(bf16[32,4096]{1,0:T(8,128)(2,1)S(1)} %fusion.6), channel_id=1, source_target_pairs={{0,2},{1,3},{2,0},{3,1},{4,6},{5,7},{6,4},{7,5},{8,10},{9,11},{10,... | collective-permute-start | bytes 786440 | tf_op jit(solution)/shard_map/ppermute | solution.py:260
  71.9 7.0 %collective-permute-start.14 = (bf16[32,4096]{1,0:T(8,128)(2,1)S(1)}, bf16[32,4096]{1,0:T(8,128)(2,1)S(1)}, u32[]{:S(2)}, u32[]{:S(2)}) collective-permute-start(bf16[32,4096]{1,0:T(8,128)(2,1)S(1)} %fusion.8), channel_id=1, source_target_pairs={{0,16},{16,0},{1,17},{17,1},{2,18},{18,2},{3,19},{19,3},{4,20},{20... | collective-permute-start | bytes 786440 | tf_op jit(solution)/shard_map/ppermute | solution.py:260
  79.1 6.5 %collective-permute-start.16 = (bf16[8,8192]{1,0:T(8,128)(2,1)S(1)}, bf16[8,8192]{1,0:T(8,128)(2,1)S(1)}, u32[]{:S(2)}, u32[]{:S(2)}) collective-permute-start(bf16[8,8192]{1,0:T(8,128)(2,1)S(1)} %slice.131.refs_1_), channel_id=1, source_target_pairs={{0,4},{1,5},{2,6},{3,7},{4,0},{5,1},{6,2},{7,3},{8,12},{9,13},{10,... | collective-permute-start | bytes 393224 | tf_op jit(solution)/shard_map/ppermute | solution.py:260
  80.3 14.5 %collective-permute-start.15 = (bf16[8,8192]{1,0:T(8,128)(2,1)S(1)}, bf16[8,8192]{1,0:T(8,128)(2,1)S(1)}, u32[]{:S(2)}, u32[]{:S(2)}) collective-permute-start(bf16[8,8192]{1,0:T(8,128)(2,1)S(1)} %slice.129.refs_2_), channel_id=1, source_target_pairs={{0,4},{1,5},{2,6},{3,7},{4,0},{5,1},{6,2},{7,3},{8,12},{9,13},{10,... | collective-permute-start | bytes 393224 | tf_op jit(solution)/shard_map/ppermute | solution.py:260
  85.7 9.1 %collective-permute-start.18 = (bf16[8,8192]{1,0:T(8,128)(2,1)S(1)}, bf16[8,8192]{1,0:T(8,128)(2,1)S(1)}, u32[]{:S(2)}, u32[]{:S(2)}) collective-permute-start(bf16[8,8192]{1,0:T(8,128)(2,1)S(1)} %fusion.10.rest_0_), channel_id=1, source_target_pairs={{0,8},{1,9},{2,10},{3,11},{4,12},{5,13},{6,14},{7,15},{8,0},{9,1},... | collective-permute-start | bytes 393224 | tf_op jit(solution)/shard_map/ppermute | solution.py:260
where the time goes:
time: 95.8 us; the launch traced here: 95.5 us
  waiting for transfers between devices  41.7 us (44%)
  starting transfers between devices  25.8 us (27%)
  Pallas kernels  20.5 us (21%)
  other arithmetic  3.32 us (3%)
  local copies, waits for them, and re-layouts  3.26 us (3%)
    ppermute x19, waiting for transfers between devices, partner(): lax.ppermute(block, axis, [(i, i ^ mask) for i in range(lax.axis_size(axi...  41.7 us
    ppermute x19, starting transfers between devices, partner(): lax.ppermute(block, axis, [(i, i ^ mask) for i in range(lax.axis_size(axi...  25.8 us
    pallas_call x2, Pallas kernels, weight_gradient(): pl.pallas_call(functools.partial(weight_kernel, first, scaled), out_shape...  8.01 us
    pallas_call x1, Pallas kernels, on_device(): pl.pallas_call(hidden_kernel, out_shape=[jax.ShapeDtypeStruct((units, row...  3.98 us
    pallas_call x1, Pallas kernels, on_device(): pl.pallas_call(factor_kernel, out_shape=jax.ShapeDtypeStruct((3 * units,...  2.65 us
    unnamed x6, local copies, waits for them, and re-layouts  2.38 us
    pallas_call x1, Pallas kernels, on_device(): pl.pallas_call(functools.partial(part_kernel, experts), out_shape=[row_ty...  2.03 us
    pallas_call x2, Pallas kernels, stage(): pl.pallas_call(stage_kernel, out_shape=jax.ShapeDtypeStruct(weight.shape,...  1.97 us
  transfers between devices with their start and end apart: 19, of which 11 were waited for; matrix products, arithmetic and copies ran while one was open for 2% of the time, Pallas kernels for 20%

commit v1 on v0

--- a/solution.py
+++ b/solution.py
@@ -419,7 +419,6 @@
         cost_estimate=cost(product, 2 * dim * (units + rows_all)),
         name="factors",
     )(ya, yb, act, silu, slope, gate, wdown, mixed_send)
-    far_factors = partner(factors, ("expert", half_axis))
     mixed_got = partner(mixed_send, core)
     back_keep, back_send = pl.pallas_call(
         back_kernel,
@@ -485,6 +484,9 @@
         if k > 0:
             mixed_got = mixed_got + zero_after(dim, back_sent)
         mixed_keep, mixed_got, mixed_sent = plane_step(mixed_keep, mixed_got, across_first, k)
+        if k == 0:
+            behind_mixed = factors + zero_after(rows_all, mixed_sent)
+            far_factors = partner(behind_mixed, ("expert", half_axis))
         back_keep, back_got, back_sent = plane_step(back_keep, back_got, near_first, k)
     both = jnp.concatenate([add(mixed_keep, mixed_got), add(back_keep, back_got)], axis=1)
     for group in groups[:0:-1]:

time: 95.8 us -> 97.5 us (1.018)
  waiting for transfers between devices: 41.7 us -> 44.8 us
  starting transfers between devices: 25.8 us -> 24.3 us
    ppermute x19, waiting for transfers between devices: 41.7 us -> 44.8 us  [partner(): lax.ppermute(block, axis, [(i, i ^ mask) for i in range(lax.axis_size(axi...]
    ppermute x19, starting transfers between devices: 25.8 us -> 24.3 us  [partner(): lax.ppermute(block, axis, [(i, i ^ mask) for i in range(lax.axis_size(axi...]
  transfers between devices with their start and end apart: 19 -> 19, of which waited for: 11 -> 12; matrix products, arithmetic and copies ran while one was open for 2% -> 2% of each run, Pallas kernels for 20% -> 19%
where the time goes in v1:
time: 97.5 us; the launch traced here: 97.2 us
  waiting for transfers between devices  44.8 us (46%)
  starting transfers between devices  24.3 us (25%)
  Pallas kernels  20.5 us (21%)
  other arithmetic  3.37 us (3%)
  local copies, waits for them, and re-layouts  3.28 us (3%)
    ppermute x19, waiting for transfers between devices, partner(): lax.ppermute(block, axis, [(i, i ^ mask) for i in range(lax.axis_size(axi...  44.8 us
    ppermute x19, starting transfers between devices, partner(): lax.ppermute(block, axis, [(i, i ^ mask) for i in range(lax.axis_size(axi...  24.3 us
    pallas_call x2, Pallas kernels, weight_gradient(): pl.pallas_call(functools.partial(weight_kernel, first, scaled), out_shape...  8.01 us
    pallas_call x1, Pallas kernels, on_device(): pl.pallas_call(hidden_kernel, out_shape=[jax.ShapeDtypeStruct((units, row...  3.98 us
    pallas_call x1, Pallas kernels, on_device(): pl.pallas_call(factor_kernel, out_shape=jax.ShapeDtypeStruct((3 * units,...  2.65 us
    unnamed x6, local copies, waits for them, and re-layouts  2.38 us
    pallas_call x1, Pallas kernels, on_device(): pl.pallas_call(functools.partial(part_kernel, experts), out_shape=[row_ty...  2.03 us
    pallas_call x2, Pallas kernels, stage(): pl.pallas_call(stage_kernel, out_shape=jax.ShapeDtypeStruct(weight.shape,...  1.97 us
  transfers between devices with their start and end apart: 19, of which 12 were waited for; matrix products, arithmetic and copies ran while one was open for 2% of the time, Pallas kernels for 19%

profile of v1, /device:TPU:0, one launch (start us, length us, event | category | flops | bytes accessed | tf_op | source)
XLA Modules:
  0.0 97.2 jit_solution(10047909595076294188)
XLA Ops:
  2.4 4.1 %collective-permute-start = (bf16[16,4224]{1,0:T(8,128)(2,1)S(1)}, bf16[16,4224]{1,0:T(8,128)(2,1)S(1)}, u32[]{:S(2)}, u32[]{:S(2)}) collective-permute-start(bf16[16,4224]{1,0:T(8,128)(2,1)S(1)} %maximum_bitcast_fusion.2), channel_id=1, source_target_pairs={{0,8},{1,9},{2,10},{3,11},{4,12},{5,13},{6,14},{7,15},{8,0},{9,1},... | collective-permute-start | bytes 405512 | tf_op jit(solution)/shard_map/ppermute | solution.py:260
  8.1 5.0 %collective-permute-done = bf16[16,4224]{1,0:T(8,128)(2,1)S(1)} collective-permute-done((bf16[16,4224]{1,0:T(8,128)(2,1)S(1)}, bf16[16,4224]{1,0:T(8,128)(2,1)S(1)}, u32[]{:S(2)}, u32[]{:S(2)}) %collective-permute-start) | collective-permute-done | bytes 135200 | tf_op jit(solution)/shard_map/ppermute | solution.py:260
  13.7 4.4 %collective-permute-done.1 = bf16[16,4224]{1,0:T(8,128)(2,1)S(1)} collective-permute-done((bf16[16,4224]{1,0:T(8,128)(2,1)S(1)}, bf16[16,4224]{1,0:T(8,128)(2,1)S(1)}, u32[]{:S(2)}, u32[]{:S(2)}) %collective-permute-start.1) | collective-permute-done | bytes 135200 | tf_op jit(solution)/shard_map/ppermute | solution.py:260
  18.3 1.6 %collective-permute-start.3 = (bf16[32,4224]{1,0:T(8,128)(2,1)S(1)}, bf16[32,4224]{1,0:T(8,128)(2,1)S(1)}, u32[]{:S(2)}, u32[]{:S(2)}) collective-permute-start(bf16[32,4224]{1,0:T(8,128)(2,1)S(1)} %bitcast.73), channel_id=1, source_target_pairs={{0,2},{1,3},{2,0},{3,1},{4,6},{5,7},{6,4},{7,5},{8,10},{9,11},{10,... | collective-permute-start | bytes 811016 | tf_op jit(solution)/shard_map/ppermute | solution.py:260
  21.4 3.4 %collective-permute-done.3 = bf16[32,4224]{1,0:T(8,128)(2,1)S(1)} collective-permute-done((bf16[32,4224]{1,0:T(8,128)(2,1)S(1)}, bf16[32,4224]{1,0:T(8,128)(2,1)S(1)}, u32[]{:S(2)}, u32[]{:S(2)}) %collective-permute-start.3) | collective-permute-done | bytes 270368 | tf_op jit(solution)/shard_map/ppermute | solution.py:260
  24.9 1.6 %collective-permute-start.4 = (bf16[64,4224]{1,0:T(8,128)(2,1)S(1)}, bf16[64,4224]{1,0:T(8,128)(2,1)S(1)}, u32[]{:S(2)}, u32[]{:S(2)}) collective-permute-start(bf16[64,4224]{1,0:T(8,128)(2,1)S(1)} %maximum_bitcast_fusion.1.refs_0_), channel_id=1, source_target_pairs={{0,16},{16,0},{1,17},{17,1},{2,18},{18,2},{3,19},{19,3},{4,20},{20... | collective-permute-start | bytes 1622024 | tf_op jit(solution)/shard_map/ppermute | solution.py:260
  26.5 2.1 %collective-permute-done.5 = bf16[32,4224]{1,0:T(8,128)(2,1)S(1)} collective-permute-done((bf16[32,4224]{1,0:T(8,128)(2,1)S(1)}, bf16[32,4224]{1,0:T(8,128)(2,1)S(1)}, u32[]{:S(2)}, u32[]{:S(2)}) %collective-permute-start.5) | collective-permute-done | bytes 270368 | tf_op jit(solution)/shard_map/ppermute | solution.py:260
  29.2 2.4 %copy-done = bf16[1,2,384,4096]{3,2,1,0:T(8,128)(2,1)S(1)} copy-done((bf16[1,2,384,4096]{3,2,1,0:T(8,128)(2,1)S(1)}, bf16[1,2,384,4096]{3,2,1,0:T(8,128)(2,1)}, u32[]{:S(2)}) %copy-start) | copy-done | bytes 6291480
  33.2 4.8 %collective-permute-done.4 = bf16[64,4224]{1,0:T(8,128)(2,1)S(1)} collective-permute-done((bf16[64,4224]{1,0:T(8,128)(2,1)S(1)}, bf16[64,4224]{1,0:T(8,128)(2,1)S(1)}, u32[]{:S(2)}, u32[]{:S(2)}) %collective-permute-start.4) | collective-permute-done | bytes 540704 | tf_op jit(solution)/shard_map/ppermute | solution.py:260
  38.9 2.0 %collective-permute-done.6.xb.rb = bf16[128,4224]{1,0:T(8,128)(2,1)S(1)} collective-permute-done((bf16[128,4224]{1,0:T(8,128)(2,1)S(1)}, bf16[128,4224]{1,0:T(8,128)(2,1)S(1)}, u32[]{:S(2)}, u32[]{:S(2)}) %collective-permute-start.6) | collective-permute-done | bytes 1081376 | tf_op jit(solution)/shard_map/ppermute | solution.py:260
  40.9 4.0 %hidden.1 = (bf16[384,256]{1,0:T(8,128)(2,1)S(1)}, f32[384,256]{1,0:T(8,128)S(1)}, f32[384,256]{1,0:T(8,128)S(1)}) custom-call(bf16[128,4224]{1,0:T(8,128)(2,1)S(1)} %maximum_bitcast_fusion.xa.ra, bf16[128,4224]{1,0:T(8,128)(2,1)S(1)} %collective-permute-done.6.xb.rb, bf16[768,4096]{1,0:T(8,128)(2,1)S(1)} %stage_in.1.refs_0_.win, ...), custom_call_target="tpu_custom_call" | custom-call | flops 1610612736 | bytes 10485760 | tf_op jit(solution)/shard_map/hidden/pallas_call | solution.py:376
  44.9 2.0 %part.1 = (bf16[128,4096]{1,0:T(8,128)(2,1)S(1)}, bf16[128,4096]{1,0:T(8,128)(2,1)S(1)}, f32[256,128]{1,0:T(8,128)S(1)}, f32[256,128]{1,0:T(8,128)S(1)}) custom-call(s32[16]{0:T(128)S(1)} %copy-done.2, bf16[128,4224]{1,0:T(8,128)(2,1)S(1)} %maximum_bitcast_fusion.xa.ra, bf16[128,4224]{1,0:T(8,128)(2,1)S(1)} %collective-permute-done.6.xb.rb, ...), custom_call_target="tpu_custom_call" | custom-call | flops 805306368 | bytes 5242880 | tf_op jit(solution)/shard_map/part/pallas_call | solution.py:394
  47.1 2.6 %factors.1.own = bf16[1152,256]{1,0:T(8,128)(2,1)S(1)} custom-call(bf16[128,4224]{1,0:T(8,128)(2,1)S(1)} %bitcast.62, bf16[128,4224]{1,0:T(8,128)(2,1)S(1)} %collective-permute-done.10.yb.rb, bf16[384,256]{1,0:T(8,128)(2,1)S(1)} %get-tuple-element.13.act, f32[384,256]{1,0:T(8,128)S(1)} %get-tuple-element.16.silu, f32[384,256]{1,0:T(8,128)S(1)} %get-tuple-element.17.slope, ...), custom_call_target="tpu_custom_call" | custom-call | flops 805306368 | bytes 5242880 | tf_op jit(solution)/shard_map/factors/pallas_call | solution.py:408
  49.8 1.8 %back.1 = (bf16[128,4096]{1,0:T(8,128)(2,1)S(1)}, bf16[128,4096]{1,0:T(8,128)(2,1)S(1)}) custom-call(bf16[1152,256]{1,0:T(8,128)(2,1)S(1)} %factors.1.own, bf16[768,4096]{1,0:T(8,128)(2,1)S(1)} %stage_in.1.refs_0_.win, bf16[128,4096]{1,0:T(8,128)(2,1)S(1)} %collective-permute-done.7.after), custom_call_target="tpu_custom_call" | custom-call | flops 1610612736 | bytes 10485760 | tf_op jit(solution)/shard_map/back/pallas_call | solution.py:423
  54.0 3.9 %collective-permute-start.17 = (bf16[1152,256]{1,0:T(8,128)(2,1)S(1)}, bf16[1152,256]{1,0:T(8,128)(2,1)S(1)}, u32[]{:S(2)}, u32[]{:S(2)}) collective-permute-start(bf16[1152,256]{1,0:T(8,128)(2,1)S(1)} %broadcast_add_fusion), channel_id=1, source_target_pairs={{0,8},{1,9},{2,10},{3,11},{4,12},{5,13},{6,14},{7,15},{8,0},{9,1},... | collective-permute-start | bytes 1769480 | tf_op jit(solution)/shard_map/ppermute | solution.py:260
  59.7 6.7 %collective-permute-done.8 = bf16[64,4096]{1,0:T(8,128)(2,1)S(1)} collective-permute-done((bf16[64,4096]{1,0:T(8,128)(2,1)S(1)}, bf16[64,4096]{1,0:T(8,128)(2,1)S(1)}, u32[]{:S(2)}, u32[]{:S(2)}) %collective-permute-start.8) | collective-permute-done | bytes 524320 | tf_op jit(solution)/shard_map/ppermute | solution.py:260
  67.2 5.8 %collective-permute-done.13 = bf16[64,4096]{1,0:T(8,128)(2,1)S(1)} collective-permute-done((bf16[64,4096]{1,0:T(8,128)(2,1)S(1)}, bf16[64,4096]{1,0:T(8,128)(2,1)S(1)}, u32[]{:S(2)}, u32[]{:S(2)}) %collective-permute-start.13) | collective-permute-done | bytes 524320 | tf_op jit(solution)/shard_map/ppermute | solution.py:260
  73.7 3.5 %collective-permute-done.12 = bf16[32,4096]{1,0:T(8,128)(2,1)S(1)} collective-permute-done((bf16[32,4096]{1,0:T(8,128)(2,1)S(1)}, bf16[32,4096]{1,0:T(8,128)(2,1)S(1)}, u32[]{:S(2)}, u32[]{:S(2)}) %collective-permute-start.12) | collective-permute-done | bytes 262176 | tf_op jit(solution)/shard_map/ppermute | solution.py:260
  77.3 2.2 %collective-permute-done.14 = bf16[32,4096]{1,0:T(8,128)(2,1)S(1)} collective-permute-done((bf16[32,4096]{1,0:T(8,128)(2,1)S(1)}, bf16[32,4096]{1,0:T(8,128)(2,1)S(1)}, u32[]{:S(2)}, u32[]{:S(2)}) %collective-permute-start.14) | collective-permute-done | bytes 262176 | tf_op jit(solution)/shard_map/ppermute | solution.py:260
  81.9 2.1 %collective-permute-done.17.refs_0_.away = bf16[1152,256]{1,0:T(8,128)(2,1)S(1)} collective-permute-done((bf16[1152,256]{1,0:T(8,128)(2,1)S(1)}, bf16[1152,256]{1,0:T(8,128)(2,1)S(1)}, u32[]{:S(2)}, u32[]{:S(2)}) %collective-permute-start.17) | collective-permute-done | bytes 589856 | tf_op jit(solution)/shard_map/ppermute | solution.py:260
  84.1 2.7 %collective-permute-done.16 = bf16[8,8192]{1,0:T(8,128)(2,1)S(1)} collective-permute-done((bf16[8,8192]{1,0:T(8,128)(2,1)S(1)}, bf16[8,8192]{1,0:T(8,128)(2,1)S(1)}, u32[]{:S(2)}, u32[]{:S(2)}) %collective-permute-start.16) | collective-permute-done | bytes 131104 | tf_op jit(solution)/shard_map/ppermute | solution.py:260
  86.8 1.6 %collective-permute-start.18 = (bf16[8,8192]{1,0:T(8,128)(2,1)S(1)}, bf16[8,8192]{1,0:T(8,128)(2,1)S(1)}, u32[]{:S(2)}, u32[]{:S(2)}) collective-permute-start(bf16[8,8192]{1,0:T(8,128)(2,1)S(1)} %fusion.10.rest_0_), channel_id=1, source_target_pairs={{0,8},{1,9},{2,10},{3,11},{4,12},{5,13},{6,14},{7,15},{8,0},{9,1},... | collective-permute-start | bytes 393224 | tf_op jit(solution)/shard_map/ppermute | solution.py:260
  88.5 3.7 %grad_down.1 = bf16[1,384,4096]{2,1,0:T(8,128)(2,1)} custom-call(s32[16]{0:T(128)S(1)} %copy-done.2, bf16[1152,256]{1,0:T(8,128)(2,1)S(1)} %factors.1.own, bf16[1152,256]{1,0:T(8,128)(2,1)S(1)} %collective-permute-done.17.refs_0_.away, f32[256,128]{1,0:T(8,128)S(1)} %get-tuple-element.21.gate, bf16[128,4224]{1,0:T(8,128)(2,1)S(1)} %bitcast.63, ...), custom_call_target="tpu_custom_call" | custom-call | flops 805306368 | bytes 5242880 | tf_op jit(solution)/shard_map/grad_down/pallas_call | solution.py:465
  92.2 4.3 %grad_in.1 = bf16[2,384,4096]{2,1,0:T(8,128)(2,1)} custom-call(s32[16]{0:T(128)S(1)} %copy-done.2, bf16[1152,256]{1,0:T(8,128)(2,1)S(1)} %factors.1.own, bf16[1152,256]{1,0:T(8,128)(2,1)S(1)} %collective-permute-done.17.refs_0_.away, f32[256,128]{1,0:T(8,128)S(1)} %get-tuple-element.21.gate, bf16[128,4224]{1,0:T(8,128)(2,1)S(1)} %maximum_bitcast_fusion.xa.ra, ...), custom_call_target="tpu_custom_call" | custom-call | flops 1610612736 | bytes 8388608 | tf_op jit(solution)/shard_map/grad_in/pallas_call | solution.py:465
  (63 shorter events, 17.8 us)
Async XLA Ops:
  2.4 10.7 %collective-permute-start = (bf16[16,4224]{1,0:T(8,128)(2,1)S(1)}, bf16[16,4224]{1,0:T(8,128)(2,1)S(1)}, u32[]{:S(2)}, u32[]{:S(2)}) collective-permute-start(bf16[16,4224]{1,0:T(8,128)(2,1)S(1)} %maximum_bitcast_fusion.2), channel_id=1, source_target_pairs={{0,8},{1,9},{2,10},{3,11},{4,12},{5,13},{6,14},{7,15},{8,0},{9,1},... | collective-permute-start | bytes 405512 | tf_op jit(solution)/shard_map/ppermute | solution.py:260
  6.5 7.2 %collective-permute-start.2 = (bf16[16,4224]{1,0:T(8,128)(2,1)S(1)}, bf16[16,4224]{1,0:T(8,128)(2,1)S(1)}, u32[]{:S(2)}, u32[]{:S(2)}) collective-permute-start(bf16[16,4224]{1,0:T(8,128)(2,1)S(1)} %maximum_bitcast_fusion.2), channel_id=1, source_target_pairs={{0,4},{1,5},{2,6},{3,7},{4,0},{5,1},{6,2},{7,3},{8,12},{9,13},{10,... | collective-permute-start | bytes 405512 | tf_op jit(solution)/shard_map/ppermute | solution.py:260
  13.1 5.0 %collective-permute-start.1 = (bf16[16,4224]{1,0:T(8,128)(2,1)S(1)}, bf16[16,4224]{1,0:T(8,128)(2,1)S(1)}, u32[]{:S(2)}, u32[]{:S(2)}) collective-permute-start(bf16[16,4224]{1,0:T(8,128)(2,1)S(1)} %collective-permute-done), channel_id=1, source_target_pairs={{0,4},{1,5},{2,6},{3,7},{4,0},{5,1},{6,2},{7,3},{8,12},{9,13},{10,... | collective-permute-start | bytes 405512 | tf_op jit(solution)/shard_map/ppermute | solution.py:260
  18.2 10.5 %copy-start.1 = (bf16[1,384,4096]{2,1,0:T(8,128)(2,1)S(1)}, bf16[1,384,4096]{2,1,0:T(8,128)(2,1)}, u32[]{:S(2)}) copy-start(bf16[1,384,4096]{2,1,0:T(8,128)(2,1)} %param.13) | copy-start | bytes 9437188
  18.3 6.5 %collective-permute-start.3 = (bf16[32,4224]{1,0:T(8,128)(2,1)S(1)}, bf16[32,4224]{1,0:T(8,128)(2,1)S(1)}, u32[]{:S(2)}, u32[]{:S(2)}) collective-permute-start(bf16[32,4224]{1,0:T(8,128)(2,1)S(1)} %bitcast.73), channel_id=1, source_target_pairs={{0,2},{1,3},{2,0},{3,1},{4,6},{5,7},{6,4},{7,5},{8,10},{9,11},{10,... | collective-permute-start | bytes 811016 | tf_op jit(solution)/shard_map/ppermute | solution.py:260
  19.9 8.6 %collective-permute-start.5 = (bf16[32,4224]{1,0:T(8,128)(2,1)S(1)}, bf16[32,4224]{1,0:T(8,128)(2,1)S(1)}, u32[]{:S(2)}, u32[]{:S(2)}) collective-permute-start(bf16[32,4224]{1,0:T(8,128)(2,1)S(1)} %bitcast.81), channel_id=1, source_target_pairs={{0,16},{16,0},{1,17},{17,1},{2,18},{18,2},{3,19},{19,3},{4,20},{20... | collective-permute-start | bytes 811016 | tf_op jit(solution)/shard_map/ppermute | solution.py:260
  24.9 13.1 %collective-permute-start.4 = (bf16[64,4224]{1,0:T(8,128)(2,1)S(1)}, bf16[64,4224]{1,0:T(8,128)(2,1)S(1)}, u32[]{:S(2)}, u32[]{:S(2)}) collective-permute-start(bf16[64,4224]{1,0:T(8,128)(2,1)S(1)} %maximum_bitcast_fusion.1.refs_0_), channel_id=1, source_target_pairs={{0,16},{16,0},{1,17},{17,1},{2,18},{18,2},{3,19},{19,3},{4,20},{20... | collective-permute-start | bytes 1622024 | tf_op jit(solution)/shard_map/ppermute | solution.py:260
  28.7 9.5 %collective-permute-start.9 = (bf16[64,4224]{1,0:T(8,128)(2,1)S(1)}, bf16[64,4224]{1,0:T(8,128)(2,1)S(1)}, u32[]{:S(2)}, u32[]{:S(2)}) collective-permute-start(bf16[64,4224]{1,0:T(8,128)(2,1)S(1)} %get-tuple-element.27.refs_1_), channel_id=1, source_target_pairs={{0,2},{1,3},{2,0},{3,1},{4,6},{5,7},{6,4},{7,5},{8,10},{9,11},{10,... | collective-permute-start | bytes 1622024 | tf_op jit(solution)/shard_map/ppermute | solution.py:260
  28.7 2.8 %copy-start = (bf16[1,2,384,4096]{3,2,1,0:T(8,128)(2,1)S(1)}, bf16[1,2,384,4096]{3,2,1,0:T(8,128)(2,1)}, u32[]{:S(2)}) copy-start(bf16[1,2,384,4096]{3,2,1,0:T(8,128)(2,1)} %param.12) | copy-start | bytes 18874372
  38.1 2.8 %collective-permute-start.6 = (bf16[128,4224]{1,0:T(8,128)(2,1)S(1)}, bf16[128,4224]{1,0:T(8,128)(2,1)S(1)}, u32[]{:S(2)}, u32[]{:S(2)}) collective-permute-start(bf16[128,4224]{1,0:T(8,128)(2,1)S(1)} %maximum_bitcast_fusion.xa.ra), channel_id=1, source_target_pairs={{0,1},{1,0},{2,3},{3,2},{4,5},{5,4},{6,7},{7,6},{8,9},{9,8},{10,11... | collective-permute-start | bytes 3244040 | tf_op jit(solution)/shard_map/ppermute | solution.py:260
  38.3 6.6 %copy-start.2 = (s32[16]{0:T(128)S(1)}, s32[16]{0:T(128)}, u32[]{:S(2)}) copy-start(s32[16]{0:T(128)} %flags.5) | copy-start | bytes 196
  38.3 8.8 %collective-permute-start.10 = (bf16[128,4224]{1,0:T(8,128)(2,1)S(1)}, bf16[128,4224]{1,0:T(8,128)(2,1)S(1)}, u32[]{:S(2)}, u32[]{:S(2)}) collective-permute-start(bf16[128,4224]{1,0:T(8,128)(2,1)S(1)} %bitcast.61), channel_id=1, source_target_pairs={{0,1},{1,0},{2,3},{3,2},{4,5},{5,4},{6,7},{7,6},{8,9},{9,8},{10,11... | collective-permute-start | bytes 3244040 | tf_op jit(solution)/shard_map/ppermute | solution.py:260
  46.9 2.9 %collective-permute-start.7 = (bf16[128,4096]{1,0:T(8,128)(2,1)S(1)}, bf16[128,4096]{1,0:T(8,128)(2,1)S(1)}, u32[]{:S(2)}, u32[]{:S(2)}) collective-permute-start(bf16[128,4096]{1,0:T(8,128)(2,1)S(1)} %get-tuple-element.15.after), channel_id=1, source_target_pairs={{0,1},{1,0},{2,3},{3,2},{4,5},{5,4},{6,7},{7,6},{8,9},{9,8},{10,11... | collective-permute-start | bytes 3145736 | tf_op jit(solution)/shard_map/ppermute | solution.py:260
  51.6 6.3 %collective-permute-start.11 = (bf16[128,4096]{1,0:T(8,128)(2,1)S(1)}, bf16[128,4096]{1,0:T(8,128)(2,1)S(1)}, u32[]{:S(2)}, u32[]{:S(2)}) collective-permute-start(bf16[128,4096]{1,0:T(8,128)(2,1)S(1)} %get-tuple-element.20), channel_id=1, source_target_pairs={{0,1},{1,0},{2,3},{3,2},{4,5},{5,4},{6,7},{7,6},{8,9},{9,8},{10,11... | collective-permute-start | bytes 3145736 | tf_op jit(solution)/shard_map/ppermute | solution.py:260
  52.3 14.0 %collective-permute-start.8 = (bf16[64,4096]{1,0:T(8,128)(2,1)S(1)}, bf16[64,4096]{1,0:T(8,128)(2,1)S(1)}, u32[]{:S(2)}, u32[]{:S(2)}) collective-permute-start(bf16[64,4096]{1,0:T(8,128)(2,1)S(1)} %get-tuple-element.23.refs_0_), channel_id=1, source_target_pairs={{0,16},{16,0},{1,17},{17,1},{2,18},{18,2},{3,19},{19,3},{4,20},{20... | collective-permute-start | bytes 1572872 | tf_op jit(solution)/shard_map/ppermute | solution.py:260
  54.0 30.0 %collective-permute-start.17 = (bf16[1152,256]{1,0:T(8,128)(2,1)S(1)}, bf16[1152,256]{1,0:T(8,128)(2,1)S(1)}, u32[]{:S(2)}, u32[]{:S(2)}) collective-permute-start(bf16[1152,256]{1,0:T(8,128)(2,1)S(1)} %broadcast_add_fusion), channel_id=1, source_target_pairs={{0,8},{1,9},{2,10},{3,11},{4,12},{5,13},{6,14},{7,15},{8,0},{9,1},... | collective-permute-start | bytes 1769480 | tf_op jit(solution)/shard_map/ppermute | solution.py:260
  58.1 14.9 %collective-permute-start.13 = (bf16[64,4096]{1,0:T(8,128)(2,1)S(1)}, bf16[64,4096]{1,0:T(8,128)(2,1)S(1)}, u32[]{:S(2)}, u32[]{:S(2)}) collective-permute-start(bf16[64,4096]{1,0:T(8,128)(2,1)S(1)} %bitcast.68), channel_id=1, source_target_pairs={{0,2},{1,3},{2,0},{3,1},{4,6},{5,7},{6,4},{7,5},{8,10},{9,11},{10,... | collective-permute-start | bytes 1572872 | tf_op jit(solution)/shard_map/ppermute | solution.py:260
  66.5 10.7 %collective-permute-start.12 = (bf16[32,4096]{1,0:T(8,128)(2,1)S(1)}, bf16[32,4096]{1,0:T(8,128)(2,1)S(1)}, u32[]{:S(2)}, u32[]{:S(2)}) collective-permute-start(bf16[32,4096]{1,0:T(8,128)(2,1)S(1)} %fusion.6), channel_id=1, source_target_pairs={{0,2},{1,3},{2,0},{3,1},{4,6},{5,7},{6,4},{7,5},{8,10},{9,11},{10,... | collective-permute-start | bytes 786440 | tf_op jit(solution)/shard_map/ppermute | solution.py:260
  73.0 6.4 %collective-permute-start.14 = (bf16[32,4096]{1,0:T(8,128)(2,1)S(1)}, bf16[32,4096]{1,0:T(8,128)(2,1)S(1)}, u32[]{:S(2)}, u32[]{:S(2)}) collective-permute-start(bf16[32,4096]{1,0:T(8,128)(2,1)S(1)} %fusion.8), channel_id=1, source_target_pairs={{0,16},{16,0},{1,17},{17,1},{2,18},{18,2},{3,19},{19,3},{4,20},{20... | collective-permute-start | bytes 786440 | tf_op jit(solution)/shard_map/ppermute | solution.py:260
  79.7 7.1 %collective-permute-start.16 = (bf16[8,8192]{1,0:T(8,128)(2,1)S(1)}, bf16[8,8192]{1,0:T(8,128)(2,1)S(1)}, u32[]{:S(2)}, u32[]{:S(2)}) collective-permute-start(bf16[8,8192]{1,0:T(8,128)(2,1)S(1)} %slice.135.refs_1_), channel_id=1, source_target_pairs={{0,4},{1,5},{2,6},{3,7},{4,0},{5,1},{6,2},{7,3},{8,12},{9,13},{10,... | collective-permute-start | bytes 393224 | tf_op jit(solution)/shard_map/ppermute | solution.py:260
  81.2 15.3 %collective-permute-start.15 = (bf16[8,8192]{1,0:T(8,128)(2,1)S(1)}, bf16[8,8192]{1,0:T(8,128)(2,1)S(1)}, u32[]{:S(2)}, u32[]{:S(2)}) collective-permute-start(bf16[8,8192]{1,0:T(8,128)(2,1)S(1)} %slice.133.refs_2_), channel_id=1, source_target_pairs={{0,4},{1,5},{2,6},{3,7},{4,0},{5,1},{6,2},{7,3},{8,12},{9,13},{10,... | collective-permute-start | bytes 393224 | tf_op jit(solution)/shard_map/ppermute | solution.py:260
  86.8 9.7 %collective-permute-start.18 = (bf16[8,8192]{1,0:T(8,128)(2,1)S(1)}, bf16[8,8192]{1,0:T(8,128)(2,1)S(1)}, u32[]{:S(2)}, u32[]{:S(2)}) collective-permute-start(bf16[8,8192]{1,0:T(8,128)(2,1)S(1)} %fusion.10.rest_0_), channel_id=1, source_target_pairs={{0,8},{1,9},{2,10},{3,11},{4,12},{5,13},{6,14},{7,15},{8,0},{9,1},... | collective-permute-start | bytes 393224 | tf_op jit(solution)/shard_map/ppermute | solution.py:260
